TPU v7x, 32 devices: a whole 2x2x4 slice. The times are simulated.
32 devices in a mesh: clip: 2 (over x), seq: 16 (over z, y, core).
Axes of the slice: x: 2, y: 2, z: 4, core: 2. Of those that a mesh axis runs over, the one named last changes fastest.
Arguments:
- spatial_saved: bfloat16 [3, 32, 256, 576], P(None, ('clip', 'seq')), parts along dimension 1, may hold values from -48 to 48
- hidden: bfloat16 [32, 256, 1152], P(('clip', 'seq')), parts along dimension 0, may hold values from -6 to 6
- temporal_out_grad: bfloat16 [32, 256, 576], P(('clip', 'seq')), parts along dimension 0, may hold values from -6 to 6
- stream_grad: bfloat16 [32, 256, 1152], P(('clip', 'seq')), parts along dimension 0, may hold values from -6 to 6
- modulation: float32 [1152], replicated, may hold values from -0.5 to 1
- temporal_weights: bfloat16 [1152, 1728], P('seq'), may hold values from -0.1875 to 0.1875
- spatial_weights: bfloat16 [576, 1152], P('seq'), may hold values from -0.25 to 0.25
Outputs:
- hidden_grad: bfloat16 [32, 256, 1152], P(('clip', 'seq')), parts along dimension 0
- spatial_grad: bfloat16 [3, 32, 256, 576], P(None, ('clip', 'seq')), parts along dimension 1
There are 2 independent parts, one for each index of `clip`. A program takes and returns all parts, laid end to end along the dimension named above; an argument that names none is the same for every part. Nothing has to cross between parts.
All inputs are finite; a program needn't handle non-finite values.
Results may differ from a plain program's by a relative error of at most 0.024.
Values may be sent and summed in bfloat16 or wider, within the bound.
No kernel may reach another device: no remote copies, remote signals or barrier semaphores. Data moves between devices by JAX's collectives and lax.ppermute only.
A program may use at most 64 MiB of HBM per device.

v0:
```python
import math
import jax
import jax.numpy as jnp
from jax import lax
from jax.sharding import PartitionSpec as P

HEADS = 8
HD = 72
epsilon = 1e-06


def attend_grad(query, keys, values, grad_o, form):
    key_form = form.replace("l", "m")
    scale = 1.0 / math.sqrt(query.shape[-1])
    scores = (
        jnp.einsum(
            form + "," + key_form + "->bhlm", query, keys, preferred_element_type=jnp.float32
        )
        * scale
    )
    attention = jax.nn.softmax(scores, axis=-1)
    rounded = attention.astype(jnp.bfloat16)
    output = jnp.einsum(
        "bhlm," + key_form + "->" + form, rounded, values, preferred_element_type=jnp.float32
    )
    delta = jnp.einsum(form + "," + form + "->bhl", grad_o.astype(jnp.float32), output)
    spread = jnp.einsum(
        form + "," + key_form + "->bhlm", grad_o, values, preferred_element_type=jnp.float32
    )
    dscore = (attention * (spread - delta[..., None])).astype(jnp.bfloat16)
    grad_query = jnp.einsum(
        "bhlm," + key_form + "->" + form, dscore, keys, preferred_element_type=jnp.float32
    )
    grad_keys = jnp.einsum(
        "bhlm," + form + "->" + key_form, dscore, query, preferred_element_type=jnp.float32
    )
    grad_values = jnp.einsum(
        "bhlm," + form + "->" + key_form, rounded, grad_o, preferred_element_type=jnp.float32
    )
    return (
        (grad_query * scale).astype(jnp.bfloat16),
        (grad_keys * scale).astype(jnp.bfloat16),
        grad_values.astype(jnp.bfloat16),
    )


def split_heads(block):
    return block.reshape(block.shape[:-1] + (HEADS, HD))


def merge_heads(block):
    return block.reshape(block.shape[:-2] + (HEADS * HD,))


def layer_norm(hidden, modulation):
    widened = hidden.astype(jnp.float32)
    mean_value = jnp.mean(widened, axis=-1, keepdims=True)
    centered = widened - mean_value
    inverse = lax.rsqrt(jnp.mean(centered * centered, axis=-1, keepdims=True) + epsilon)
    normal_form = centered * inverse
    normed = (normal_form * (1.0 + modulation)).astype(jnp.bfloat16)
    return (normed, normal_form, inverse)


def norm_back(grad_normed, normal_form, inverse, modulation):
    scaled = grad_normed * (1.0 + modulation)
    return inverse * (
        scaled
        - jnp.mean(scaled, axis=-1, keepdims=True)
        - normal_form * jnp.mean(scaled * normal_form, axis=-1, keepdims=True)
    )


def temporal_backward(projected, grad_patch):
    width = HEADS * HD
    grads = attend_grad(
        split_heads(projected[..., :width]),
        split_heads(projected[..., width : 2 * width]),
        split_heads(projected[..., 2 * width :]),
        split_heads(grad_patch),
        "lbhd",
    )
    return jnp.concatenate([merge_heads(gradient) for gradient in grads], axis=-1)


def shards(
    spatial_saved,
    hidden,
    temporal_out_grad,
    stream_grad,
    modulation,
    temporal_weights,
    spatial_weights,
):
    grad_patch = lax.all_to_all(temporal_out_grad, "seq", split_axis=1, concat_axis=0, tiled=True)
    hidden_patch = lax.all_to_all(hidden, "seq", split_axis=1, concat_axis=0, tiled=True)
    normed, normal_form, inverse = layer_norm(hidden_patch, modulation)
    projected = jnp.einsum(
        "fpd,dc->fpc",
        normed,
        lax.all_gather(temporal_weights, "seq", axis=0, tiled=True),
        preferred_element_type=jnp.float32,
    ).astype(jnp.bfloat16)
    projection_grads = temporal_backward(projected, grad_patch)
    branch = norm_back(
        jnp.einsum(
            "fpc,dc->fpd",
            projection_grads,
            lax.all_gather(temporal_weights, "seq", axis=0, tiled=True),
            preferred_element_type=jnp.float32,
        ),
        normal_form,
        inverse,
        modulation,
    ).astype(jnp.bfloat16)
    branch = lax.all_to_all(branch, "seq", split_axis=0, concat_axis=1, tiled=True)
    branch = lax.optimization_barrier(branch)
    hidden_grad = (stream_grad.astype(jnp.float32) + branch.astype(jnp.float32)).astype(
        jnp.bfloat16
    )
    attention_grad = jnp.einsum(
        "fpd,cd->fpc",
        hidden_grad,
        lax.all_gather(spatial_weights, "seq", axis=0, tiled=True),
        preferred_element_type=jnp.float32,
    ).astype(jnp.bfloat16)
    spatial = attend_grad(
        split_heads(spatial_saved[0]),
        split_heads(spatial_saved[1]),
        split_heads(spatial_saved[2]),
        split_heads(attention_grad),
        "blhd",
    )
    spatial_grad = jnp.stack([merge_heads(gradient) for gradient in spatial])
    return (hidden_grad, spatial_grad)


def solution(mesh):
    return jax.shard_map(
        shards,
        mesh=mesh,
        in_specs=(
            P(None, ("clip", "seq"), None, None),
            P(("clip", "seq"), None, None),
            P(("clip", "seq"), None, None),
            P(("clip", "seq"), None, None),
            P(),
            P("seq", None),
            P("seq", None),
        ),
        out_specs=(P(("clip", "seq"), None, None), P(None, ("clip", "seq"), None, None)),
        check_vma=False,
    )
```

profile of v0, /device:TPU:0, one launch (start us, length us, event | category | flops | bytes accessed | tf_op | source)
XLA Modules:
  0.0 136.8 jit_solution(4414544214536378165)
XLA Ops:
  7.2 0.7 all-gather.4.cloned.1.call-update
  7.9 1.4 %copy.61 = bf16[1,256,576]{2,0,1:T(2,128)(2,1)S(1)} copy(bf16[1,256,576]{1,2,0:T(8,128)(2,1)} %param.9) | data formatting | bytes 589824 | tf_op args[2]
  9.3 0.5 broadcast.94
  9.9 2.7 %reduce.13 = bf16[256,576]{1,0:T(8,128)(2,1)S(1)} reduce(bf16[256,1,576]{2,1,0:T(2,128)(2,1)S(1)} %bitcast.105, bf16[]{:T(256)} %broadcast.94), dimensions={1}, to_apply=%bitcast.75.reduce_sub_computation | reduce | bytes 589826
  12.6 1.1 reshape.177
  13.7 7.4 %all-to-all-start.1 = ((bf16[16,2,4608]{2,1,0:T(2,128)(2,1)}), bf16[16,2,4608]{2,1,0:T(2,128)(2,1)S(1)}, u32[]{:S(2)}, u32[]{:S(2)}) async-start(bf16[16,2,4608]{2,1,0:T(2,128)(2,1)} %reshape.177), calls=%async_computation.1 | async-start | bytes 589824 | tf_op jit(solution)/shard_map/all_to_all | solution.py:95
  21.1 0.9 copy.134
  22.0 4.2 %reduce.12 = bf16[256,1152]{1,0:T(8,128)(2,1)S(1)} reduce(bf16[256,1,1152]{2,1,0:T(2,128)(2,1)S(1)} %bitcast.101, bf16[]{:T(256)} %broadcast.94), dimensions={1}, to_apply=%bitcast.97.reduce_sub_computation | reduce | bytes 1179650
  26.2 0.9 reshape.175
  27.2 9.1 %all-to-all-done.1 = bf16[16,2,4608]{2,1,0:T(2,128)(2,1)S(1)} async-done(((bf16[16,2,4608]{2,1,0:T(2,128)(2,1)}), bf16[16,2,4608]{2,1,0:T(2,128)(2,1)S(1)}, u32[]{:S(2)}, u32[]{:S(2)}) %all-to-all-start.1) | async-done | bytes 294944 | tf_op jit(solution)/shard_map/all_to_all | solution.py:95
  36.3 4.8 %all-to-all-start = ((bf16[16,2,9216]{2,1,0:T(2,128)(2,1)}), bf16[16,2,9216]{2,1,0:T(2,128)(2,1)S(1)}, u32[]{:S(2)}, u32[]{:S(2)}) async-start(bf16[16,2,9216]{2,1,0:T(2,128)(2,1)} %reshape.175), calls=%async_computation | async-start | bytes 1179648 | tf_op jit(solution)/shard_map/all_to_all | solution.py:96
  41.3 0.5 all-gather.6.cloned.1.call-update
  41.9 0.6 reshape.178
  42.4 1.8 %bitcast_reduce_fusion = bf16[256,576]{1,0:T(8,128)(2,1)S(1)} fusion(bf16[256,1,576]{2,1,0:T(2,128)(2,1)S(1)} %reshape.178), kind=kLoop, calls=%fused_computation.78 | loop fusion | bytes 589824 | tf_op jit(solution)/shard_map/all_to_all | solution.py:95
  44.3 0.6 reshape.154
  44.8 19.4 %all-to-all-done = bf16[16,2,9216]{2,1,0:T(2,128)(2,1)S(1)} async-done(((bf16[16,2,9216]{2,1,0:T(2,128)(2,1)}), bf16[16,2,9216]{2,1,0:T(2,128)(2,1)S(1)}, u32[]{:S(2)}, u32[]{:S(2)}) %all-to-all-start) | async-done | bytes 589856 | tf_op jit(solution)/shard_map/all_to_all | solution.py:96
  64.3 0.5 reshape.176
  65.4 10.7 %all-gather.4.cloned.1.call-done = bf16[1152,1728]{1,0:T(8,128)(2,1)} async-done(((bf16[72,1728]{1,0:T(8,128)(2,1)}), bf16[1152,1728]{1,0:T(8,128)(2,1)}) %all-gather.4.cloned.1.call-update) | async-done | bytes 3981328 | tf_op jit(solution)/shard_map/all_gather | solution.py:101
  76.1 3.6 %fusion.9 = bf16[16,16,1728]{2,1,0:T(8,128)(2,1)S(1)} fusion(bf16[1152,1728]{1,0:T(8,128)(2,1)} %all-gather.4.cloned.1.call-done, f32[16,16,1152]{2,1,0:T(8,128)S(1)} %bitcast.102, f32[1152]{0:T(1024)S(1)} %broadcast_add_fusion, f32[16,16]{1,0:T(8,128)S(1)} %div.33, f32[16,16]{1,0:T(8,128)S(1)} %rsqrt.12), kind=kOutput, calls=%fused_computation.7 | convolution fusion | flops 1020837888 | bytes 6052352 | tf_op jit(solution)/shard_map/fpd,dc->fpc/dot_general | solution.py:98
  79.9 0.6 reshape.151
  80.5 0.6 reshape.152
  81.0 1.4 reshape.153
  82.4 2.0 %fusion.60 = (f32[16,8,16]{2,1,0:T(8,128)S(1)}, f32[16,8,16,16]{2,3,1,0:T(8,128)}) fusion(bf16[16,16,8,72]{3,2,1,0:T(8,128)(2,1)S(1)} %reshape.151, bf16[16,16,8,72]{3,2,1,0:T(8,128)(2,1)S(1)} %reshape.152), kind=kOutput, calls=%fused_computation.75 | convolution fusion | flops 4816911 | bytes 729088 | tf_op jit(solution)/shard_map/sub | solution.py:21
  84.4 2.7 %fusion.22 = bf16[16,16,8,72]{3,0,2,1:T(8,128)(2,1)} fusion(bf16[16,16,8,72]{3,2,1,0:T(8,128)(2,1)S(1)} %reshape.154, f32[16,8,16,16]{2,3,1,0:T(8,128)} %get-tuple-element.11, f32[16,8,16]{2,1,0:T(8,128)S(1)} %get-tuple-element.10), kind=kOutput, calls=%fused_computation.30 | convolution fusion | flops 4931584 | bytes 729088 | tf_op jit(solution)/shard_map/bhlm,lbhd->mbhd/dot_general | solution.py:37
  87.1 0.5 convolution_bitcast_fusion
  87.6 0.5 multiply_reduce_fusion.3
  88.2 2.0 %fusion.17 = bf16[16,8,16,16]{2,3,1,0:T(8,128)(2,1)S(1)} fusion(f32[16,8,16]{2,1,0:T(8,128)S(1)} %copy.85, bf16[16,16,8,72]{3,2,1,0:T(8,128)(2,1)S(1)} %reshape.154, bf16[16,16,8,72]{3,2,1,0:T(8,128)(2,1)S(1)} %copy-done.6, f32[16,8,16,16]{2,3,1,0:T(8,128)} %get-tuple-element.11, f32[16,8,16]{2,1,0:T(8,128)} %copy-done.11), kind=kOutput, calls=%fused_computation.21 | convolution fusion | flops 4849664 | bytes 802816 | tf_op jit(solution)/shard_map/lbhd,mbhd->bhlm/dot_general | solution.py:27
  90.2 0.4 fusion.20
  90.6 0.5 fusion.21
  91.1 0.5 copy-done.5
  91.8 0.4 reshape.157
  92.3 0.4 reshape.156
  93.2 1.2 concatenate.3
  94.4 3.9 %fusion.57 = (f32[16,16]{1,0:T(8,128)S(1)}, f32[16,16]{1,0:T(8,128)S(1)}, f32[16,16,1152]{2,1,0:T(8,128)S(1)}) fusion(f32[16,16]{1,0:T(8,128)S(1)} %rsqrt.12, f32[16,16,1152]{2,1,0:T(8,128)S(1)} %bitcast.103, f32[16,16]{1,0:T(8,128)S(1)} %div.33, f32[1152]{0:T(1024)S(1)} %broadcast_add_fusion, bf16[16,16,1728]{2,1,0:T(8,128)(2,1)} %concatenate.3, ...), kind=kOutput, calls=%fused_computation.72 | convolution fusion | flops 1020984832 | bytes 7234048 | tf_op jit(solution)/shard_map/fpc,dc->fpd/dot_general | solution.py:106
  98.4 1.2 multiply_convert_fusion.1
  99.6 3.8 %all-to-all-start.2 = ((bf16[16,16,1152]{2,1,0:T(8,128)(2,1)}), bf16[16,16,1152]{2,1,0:T(8,128)(2,1)S(1)}, u32[]{:S(2)}, u32[]{:S(2)}) async-start(bf16[16,16,1152]{2,1,0:T(8,128)(2,1)} %multiply_convert_fusion.1), calls=%async_computation.2 | async-start | bytes 1179648 | tf_op jit(solution)/shard_map/all_to_all | solution.py:116
  103.4 0.8 fusion.59
  104.2 2.2 %fusion.65 = (f32[8,256]{1,0:T(8,128)S(1)}, f32[8,256,256]{1,2,0:T(8,128)}) fusion(bf16[256,8,72]{0,2,1:T(8,128)(2,1)S(1)} %bitcast.107, bf16[256,8,72]{0,2,1:T(8,128)(2,1)S(1)} %bitcast.109), kind=kOutput, calls=%fused_computation.76 | convolution fusion | flops 77070592 | bytes 2695168 | tf_op jit(solution)/shard_map/sub | solution.py:21
  106.4 1.8 %fusion.27 = bf16[8,256,256]{1,2,0:T(8,128)(2,1)S(1)} fusion(f32[8,256,256]{1,2,0:T(8,128)} %get-tuple-element.14, f32[8,256]{1,0:T(8,128)S(1)} %get-tuple-element.13), kind=kLoop, calls=%fused_computation.46 | loop fusion | flops 1048576 | bytes 3153920 | tf_op jit(solution)/shard_map/convert_element_type | solution.py:22
  108.2 13.7 %all-gather.6.cloned.1.call-done = bf16[16,36,1152]{2,1,0:T(8,128)(2,1)} async-done(((bf16[1,36,1152]{2,1,0:T(8,128)(2,1)}), bf16[16,36,1152]{2,1,0:T(8,128)(2,1)}) %all-gather.6.cloned.1.call-update) | async-done | bytes 1327120 | tf_op jit(solution)/shard_map/all_gather | solution.py:124
  121.9 2.2 %reshape.166 = bf16[576,1152]{1,0:T(8,128)(2,1)S(1)} reshape(bf16[16,36,1152]{2,1,0:T(8,128)(2,1)} %all-gather.6.cloned.1.call-done) | data formatting | bytes 2654208
  124.2 1.2 add_convert_fusion
  125.4 0.6 convolution_convert_fusion.1
  126.4 0.8 copy-done
  127.2 0.5 multiply_convert_fusion
  128.1 0.5 fusion.24
  128.5 0.4 convolution_convert_fusion.2
  129.0 1.0 pad_maximum_fusion
  (42 shorter events, 2.7 us)
Async XLA Ops:
  7.2 69.0 %all-gather.4.cloned.1.call-start = ((), (), s32[]{:S(2)}) async-start(), calls=%async_computation.3 | async-start | bytes 4386816 | tf_op jit(solution)/shard_map/all_gather | solution.py:101
  9.3 11.7 %copy-start.3 = (bf16[1,256,1152]{2,1,0:T(8,128)(2,1)S(1)}, bf16[1,256,1152]{2,1,0:T(8,128)(2,1)}, u32[]{:S(2)}) copy-start(bf16[1,256,1152]{2,1,0:T(8,128)(2,1)} %param.8) | copy-start | bytes 1769476
  13.7 22.6 %all-to-all-start.1 = ((bf16[16,2,4608]{2,1,0:T(2,128)(2,1)}), bf16[16,2,4608]{2,1,0:T(2,128)(2,1)S(1)}, u32[]{:S(2)}, u32[]{:S(2)}) async-start(bf16[16,2,4608]{2,1,0:T(2,128)(2,1)} %reshape.177), calls=%async_computation.1 | async-start | bytes 589824 | tf_op jit(solution)/shard_map/all_to_all | solution.py:95
  26.2 15.6 %copy-start.9 = (f32[1152]{0:T(1024)S(1)}, f32[1152]{0:T(1024)}, u32[]{:S(2)}) copy-start(f32[1152]{0:T(1024)} %param.11) | copy-start | bytes 13828
  36.3 28.0 %all-to-all-start = ((bf16[16,2,9216]{2,1,0:T(2,128)(2,1)}), bf16[16,2,9216]{2,1,0:T(2,128)(2,1)S(1)}, u32[]{:S(2)}, u32[]{:S(2)}) async-start(bf16[16,2,9216]{2,1,0:T(2,128)(2,1)} %reshape.175), calls=%async_computation | async-start | bytes 1179648 | tf_op jit(solution)/shard_map/all_to_all | solution.py:96
  41.1 80.8 %all-gather.6.cloned.1.call-start = ((), (), s32[]{:S(2)}) async-start(), calls=%async_computation.4 | async-start | bytes 1566720 | tf_op jit(solution)/shard_map/all_gather | solution.py:124
  84.4 2.7 %copy-start.11 = (f32[16,8,16]{2,1,0:T(8,128)}, f32[16,8,16]{2,1,0:T(8,128)S(1)}, u32[]{:S(2)}) copy-start(f32[16,8,16]{2,1,0:T(8,128)S(1)} %get-tuple-element.10) | copy-start | bytes 24580
  84.4 2.7 %copy-start.6 = (bf16[16,16,8,72]{3,2,1,0:T(8,128)(2,1)S(1)}, bf16[16,16,8,72]{3,2,1,0:T(8,128)(2,1)}, u32[]{:S(2)}) copy-start(bf16[16,16,8,72]{3,2,1,0:T(8,128)(2,1)} %reshape.153) | copy-start | bytes 884740
  84.4 2.7 %copy-start.10 = (f32[16,8,16,16]{2,3,1,0:T(8,128)S(1)}, f32[16,8,16,16]{2,3,1,0:T(8,128)}, u32[]{:S(2)}) copy-start(f32[16,8,16,16]{2,3,1,0:T(8,128)} %get-tuple-element.11) | copy-start | bytes 393220
  90.6 1.0 copy-start.5
  99.6 3.8 %copy-start.2 = (bf16[3,1,256,576]{2,3,1,0:T(8,128)(2,1)S(1)}, bf16[3,1,256,576]{2,3,1,0:T(8,128)(2,1)}, u32[]{:S(2)}) copy-start(bf16[3,1,256,576]{2,3,1,0:T(8,128)(2,1)} %param.7) | copy-start | bytes 2654212
  99.6 24.6 %all-to-all-start.2 = ((bf16[16,16,1152]{2,1,0:T(8,128)(2,1)}), bf16[16,16,1152]{2,1,0:T(8,128)(2,1)S(1)}, u32[]{:S(2)}, u32[]{:S(2)}) async-start(bf16[16,16,1152]{2,1,0:T(8,128)(2,1)} %multiply_convert_fusion.1), calls=%async_computation.2 | async-start | bytes 1179648 | tf_op jit(solution)/shard_map/all_to_all | solution.py:116
  106.4 1.8 %copy-start.7 = (f32[8,256]{1,0:T(8,128)}, f32[8,256]{1,0:T(8,128)S(1)}, u32[]{:S(2)}) copy-start(f32[8,256]{1,0:T(8,128)S(1)} %get-tuple-element.13) | copy-start | bytes 24580
  124.2 1.9 %copy-start.1 = (bf16[1,1,256,576]{2,3,1,0:T(8,128)(2,1)S(1)}, bf16[1,1,256,576]{2,3,1,0:T(8,128)(2,1)}, u32[]{:S(2)}) copy-start(bf16[1,1,256,576]{2,3,1,0:T(8,128)(2,1)} %get-tuple-element.7) | copy-start | bytes 884740
  125.4 1.0 copy-start.4
  125.4 1.8 %copy-start = (f32[8,256,256]{1,2,0:T(8,128)S(1)}, f32[8,256,256]{1,2,0:T(8,128)}, u32[]{:S(2)}) copy-start(f32[8,256,256]{1,2,0:T(8,128)} %get-tuple-element.14) | copy-start | bytes 6291460
  126.0 1.2 copy-start.8
Sparse Core Ops, SparseCore 0:
  10.3 65.7 all-gather.3
  78.3 43.5 all-gather.5
where the time goes:
time: 138 us; the launch traced here: 137 us
  waiting for transfers between devices  54.1 us (39%)
  matrix products  20.4 us (15%)
  local copies, waits for them, and re-layouts  18.4 us (13%)
  starting transfers between devices  16.2 us (12%)
  between operations  14.4 us (10%)
  other arithmetic  13.2 us (10%)
    all_to_all x1, waiting for transfers between devices, shards(): lax.all_to_all(hidden, 'seq', split_axis=1, concat_axis=0, tiled=True)  19.4 us
    all_gather x1, waiting for transfers between devices, shards(): lax.all_gather(spatial_weights, 'seq', axis=0, tiled=True)  13.7 us
    all_gather x1, waiting for transfers between devices, shards(): lax.all_gather(temporal_weights, 'seq', axis=0, tiled=True)  10.7 us
    unnamed x32, local copies, waits for them, and re-layouts  9.62 us
    all_to_all x1, waiting for transfers between devices, shards(): lax.all_to_all(temporal_out_grad, 'seq', split_axis=1, concat_axis=0, til...  9.12 us
    unnamed x3, other arithmetic  7.44 us
    all_to_all x1, starting transfers between devices, shards(): lax.all_to_all(temporal_out_grad, 'seq', split_axis=1, concat_axis=0, til...  7.39 us
    all_to_all x1, starting transfers between devices, shards(): lax.all_to_all(hidden, 'seq', split_axis=1, concat_axis=0, tiled=True)  4.79 us
  transfers between devices with their start and end apart: 5, of which 4 were waited for; matrix products, arithmetic and copies ran while one was open for 33% of the time, Pallas kernels for 0%

commit v1 on v0

--- a/solution.py
+++ b/solution.py
@@ -7,6 +7,22 @@
 HEADS = 8
 HD = 72
 epsilon = 1e-06
+
+
+def swapped_with_each(shard, axis, split, join):
+    ways, here = (lax.axis_size(axis), lax.axis_index(axis))
+    width = shard.shape[split] // ways
+    lengths = list(shard.shape)
+    lengths[split] = width
+    height = lengths[join]
+    lengths[join] = height * ways
+    full = jnp.zeros(lengths, shard.dtype)
+    for mask in range(ways):
+        part = lax.dynamic_slice_in_dim(shard, (here ^ mask) * width, width, axis=split)
+        if mask:
+            part = lax.ppermute(part, axis, [(d, d ^ mask) for d in range(ways)])
+        full = lax.dynamic_update_slice_in_dim(full, part, (here ^ mask) * height, axis=join)
+    return full
 
 
 def attend_grad(query, keys, values, grad_o, form):
@@ -93,7 +109,7 @@
     spatial_weights,
 ):
     grad_patch = lax.all_to_all(temporal_out_grad, "seq", split_axis=1, concat_axis=0, tiled=True)
-    hidden_patch = lax.all_to_all(hidden, "seq", split_axis=1, concat_axis=0, tiled=True)
+    hidden_patch = swapped_with_each(hidden, "seq", 1, 0)
     normed, normal_form, inverse = layer_norm(hidden_patch, modulation)
     projected = jnp.einsum(
         "fpd,dc->fpc",

time: 138 us -> 132 us (0.957)
  starting transfers between devices: 16.2 us -> 33.2 us
  waiting for transfers between devices: 54.1 us -> 40 us
  other arithmetic: 13.2 us -> 8.93 us
  local copies, waits for them, and re-layouts: 18.4 us -> 14.4 us
    ppermute x0 -> x15, starting transfers between devices: none -> 23.2 us  [swapped_with_each(): part = lax.ppermute(part, axis, [(d, d ^ mask) for d in range(ways)])]
    all_to_all x1 -> x0, waiting for transfers between devices: 19.4 us -> none  [shards(): lax.all_to_all(hidden, 'seq', split_axis=1, concat_axis=0, tiled=True)]
    ppermute x0 -> x15, waiting for transfers between devices: none -> 11.5 us  [swapped_with_each(): part = lax.ppermute(part, axis, [(d, d ^ mask) for d in range(ways)])]
    all_to_all x1, waiting for transfers between devices: 9.12 us -> 0.01 us  [shards(): lax.all_to_all(temporal_out_grad, 'seq', split_axis=1, concat_axis=0, til...]
    all_to_all x1 -> x0, starting transfers between devices: 4.79 us -> none  [shards(): lax.all_to_all(hidden, 'seq', split_axis=1, concat_axis=0, tiled=True)]
    unnamed x3 -> x2, other arithmetic: 7.44 us -> 3.22 us
    unnamed x32 -> x29, local copies, waits for them, and re-layouts: 9.62 us -> 6.22 us
    all_gather x1, waiting for transfers between devices: 10.7 us -> 12.3 us  [shards(): lax.all_gather(temporal_weights, 'seq', axis=0, tiled=True)]
  transfers between devices with their start and end apart: 5 -> 19, of which waited for: 4 -> 7; matrix products, arithmetic and copies ran while one was open for 33% -> 29% of each run, Pallas kernels for 0% -> 0%
where the time goes in v1:
time: 132 us
  waiting for transfers between devices  40 us (30%)
  starting transfers between devices  33.2 us (25%)
  matrix products  20.4 us (15%)
  between operations  14.7 us (11%)
  local copies, waits for them, and re-layouts  14.4 us (11%)
  other arithmetic  8.93 us (7%)
    ppermute x15, starting transfers between devices, swapped_with_each(): part = lax.ppermute(part, axis, [(d, d ^ mask) for d in range(ways)])  23.2 us
    all_gather x1, waiting for transfers between devices, shards(): lax.all_gather(spatial_weights, 'seq', axis=0, tiled=True)  14.7 us
    all_gather x1, waiting for transfers between devices, shards(): lax.all_gather(temporal_weights, 'seq', axis=0, tiled=True)  12.3 us
    ppermute x15, waiting for transfers between devices, swapped_with_each(): part = lax.ppermute(part, axis, [(d, d ^ mask) for d in range(ways)])  11.5 us
    unnamed x29, local copies, waits for them, and re-layouts  6.22 us
    all_to_all x1, starting transfers between devices, shards(): lax.all_to_all(temporal_out_grad, 'seq', split_axis=1, concat_axis=0, til...  6.09 us
    sub x2, matrix products, attend_grad(): attention = jax.nn.softmax(scores, axis=-1)  4.16 us
    all_to_all x1, starting transfers between devices, shards(): lax.all_to_all(branch, 'seq', split_axis=0, concat_axis=1, tiled=True)  3.83 us
  transfers between devices with their start and end apart: 19, of which 7 were waited for; matrix products, arithmetic and copies ran while one was open for 29% of the time, Pallas kernels for 0%

profile of v1, /device:TPU:0, one launch (start us, length us, event | category | flops | bytes accessed | tf_op | source)
XLA Modules:
  0.0 131.7 jit_solution(8852103171129714610)
XLA Ops:
  7.2 0.7 all-gather.4.cloned.1.call-update
  8.3 0.5 collective-permute-start
  8.8 2.6 %collective-permute-start.1 = (bf16[1,16,1152]{2,1,0:T(8,128)(2,1)S(1)}, bf16[1,16,1152]{2,1,0:T(8,128)(2,1)S(1)}, u32[]{:S(2)}, u32[]{:S(2)}) collective-permute-start(bf16[1,16,1152]{2,1,0:T(8,128)(2,1)S(1)} %get-tuple-element.22), channel_id=1, source_target_pairs={{0,2},{1,3},{2,0},{3,1},{4,6},{5,7},{6,4},{7,5},{8,10},{9,11},{10,... | collective-permute-start | bytes 110600 | tf_op jit(solution)/shard_map/ppermute | solution.py:23
  11.5 1.8 %collective-permute-start.3 = (bf16[1,16,1152]{2,1,0:T(8,128)(2,1)S(1)}, bf16[1,16,1152]{2,1,0:T(8,128)(2,1)S(1)}, u32[]{:S(2)}, u32[]{:S(2)}) collective-permute-start(bf16[1,16,1152]{2,1,0:T(8,128)(2,1)S(1)} %get-tuple-element.20), channel_id=1, source_target_pairs={{0,4},{1,5},{2,6},{3,7},{4,0},{5,1},{6,2},{7,3},{8,12},{9,13},{10,... | collective-permute-start | bytes 110600 | tf_op jit(solution)/shard_map/ppermute | solution.py:23
  13.3 0.6 copy.39
  14.4 2.7 %reduce.10 = bf16[256,576]{1,0:T(8,128)(2,1)S(1)} reduce(bf16[256,1,576]{2,1,0:T(2,128)(2,1)S(1)} %bitcast.93, bf16[]{:T(256)} %broadcast.84), dimensions={1}, to_apply=%bitcast.72.reduce_sub_computation | reduce | bytes 589826
  17.1 1.1 reshape.159
  18.2 6.1 %all-to-all-start = ((bf16[16,2,4608]{2,1,0:T(2,128)(2,1)}), bf16[16,2,4608]{2,1,0:T(2,128)(2,1)S(1)}, u32[]{:S(2)}, u32[]{:S(2)}) async-start(bf16[16,2,4608]{2,1,0:T(2,128)(2,1)} %reshape.159), calls=%async_computation | async-start | bytes 589824 | tf_op jit(solution)/shard_map/all_to_all | solution.py:111
  24.3 0.7 all-gather.6.cloned.1.call-update
  25.2 2.9 %collective-permute-start.5 = (bf16[1,16,1152]{2,1,0:T(8,128)(2,1)S(1)}, bf16[1,16,1152]{2,1,0:T(8,128)(2,1)S(1)}, u32[]{:S(2)}, u32[]{:S(2)}) collective-permute-start(bf16[1,16,1152]{2,1,0:T(8,128)(2,1)S(1)} %get-tuple-element.18), channel_id=1, source_target_pairs={{0,6},{1,7},{2,4},{3,5},{4,2},{5,3},{6,0},{7,1},{8,14},{9,15},{10,... | collective-permute-start | bytes 110600 | tf_op jit(solution)/shard_map/ppermute | solution.py:23
  28.2 2.4 %collective-permute-start.7 = (bf16[1,16,1152]{2,1,0:T(8,128)(2,1)S(1)}, bf16[1,16,1152]{2,1,0:T(8,128)(2,1)S(1)}, u32[]{:S(2)}, u32[]{:S(2)}) collective-permute-start(bf16[1,16,1152]{2,1,0:T(8,128)(2,1)S(1)} %get-tuple-element.16), channel_id=1, source_target_pairs={{0,8},{1,9},{2,10},{3,11},{4,12},{5,13},{6,14},{7,15},{8,0},{9,1},... | collective-permute-start | bytes 110600 | tf_op jit(solution)/shard_map/ppermute | solution.py:23
  31.0 3.6 %collective-permute-start.9 = (bf16[1,16,1152]{2,1,0:T(8,128)(2,1)S(1)}, bf16[1,16,1152]{2,1,0:T(8,128)(2,1)S(1)}, u32[]{:S(2)}, u32[]{:S(2)}) collective-permute-start(bf16[1,16,1152]{2,1,0:T(8,128)(2,1)S(1)} %get-tuple-element.14), channel_id=1, source_target_pairs={{0,10},{1,11},{2,8},{3,9},{4,14},{5,15},{6,12},{7,13},{8,2},{9,3},... | collective-permute-start | bytes 110600 | tf_op jit(solution)/shard_map/ppermute | solution.py:23
  34.6 2.5 %collective-permute-done.5 = bf16[1,16,1152]{2,1,0:T(8,128)(2,1)S(1)} collective-permute-done((bf16[1,16,1152]{2,1,0:T(8,128)(2,1)S(1)}, bf16[1,16,1152]{2,1,0:T(8,128)(2,1)S(1)}, u32[]{:S(2)}, u32[]{:S(2)}) %collective-permute-start.5) | collective-permute-done | bytes 36896 | tf_op jit(solution)/shard_map/ppermute | solution.py:23
  37.1 3.4 %collective-permute-start.10 = (bf16[1,16,1152]{2,1,0:T(8,128)(2,1)S(1)}, bf16[1,16,1152]{2,1,0:T(8,128)(2,1)S(1)}, u32[]{:S(2)}, u32[]{:S(2)}) collective-permute-start(bf16[1,16,1152]{2,1,0:T(8,128)(2,1)S(1)} %get-tuple-element.13), channel_id=1, source_target_pairs={{0,11},{1,10},{2,9},{3,8},{4,15},{5,14},{6,13},{7,12},{8,3},{9,2},... | collective-permute-start | bytes 110600 | tf_op jit(solution)/shard_map/ppermute | solution.py:23
  40.5 0.5 collective-permute-start.11
  41.1 3.1 %collective-permute-done.7 = bf16[1,16,1152]{2,1,0:T(8,128)(2,1)S(1)} collective-permute-done((bf16[1,16,1152]{2,1,0:T(8,128)(2,1)S(1)}, bf16[1,16,1152]{2,1,0:T(8,128)(2,1)S(1)}, u32[]{:S(2)}, u32[]{:S(2)}) %collective-permute-start.7) | collective-permute-done | bytes 36896 | tf_op jit(solution)/shard_map/ppermute | solution.py:23
  44.2 0.8 collective-permute-start.12
  45.0 3.1 %collective-permute-start.13 = (bf16[1,16,1152]{2,1,0:T(8,128)(2,1)S(1)}, bf16[1,16,1152]{2,1,0:T(8,128)(2,1)S(1)}, u32[]{:S(2)}, u32[]{:S(2)}) collective-permute-start(bf16[1,16,1152]{2,1,0:T(8,128)(2,1)S(1)} %get-tuple-element.25), channel_id=1, source_target_pairs={{0,14},{1,15},{2,12},{3,13},{4,10},{5,11},{6,8},{7,9},{8,6},{9,7},... | collective-permute-start | bytes 110600 | tf_op jit(solution)/shard_map/ppermute | solution.py:23
  48.2 1.0 collective-permute-start.14
  49.6 2.7 %collective-permute-done.13 = bf16[1,16,1152]{2,1,0:T(8,128)(2,1)S(1)} collective-permute-done((bf16[1,16,1152]{2,1,0:T(8,128)(2,1)S(1)}, bf16[1,16,1152]{2,1,0:T(8,128)(2,1)S(1)}, u32[]{:S(2)}, u32[]{:S(2)}) %collective-permute-start.13) | collective-permute-done | bytes 36896 | tf_op jit(solution)/shard_map/ppermute | solution.py:23
  52.3 2.9 %collective-permute-done.14 = bf16[1,16,1152]{2,1,0:T(8,128)(2,1)S(1)} collective-permute-done((bf16[1,16,1152]{2,1,0:T(8,128)(2,1)S(1)}, bf16[1,16,1152]{2,1,0:T(8,128)(2,1)S(1)}, u32[]{:S(2)}, u32[]{:S(2)}) %collective-permute-start.14) | collective-permute-done | bytes 36896 | tf_op jit(solution)/shard_map/ppermute | solution.py:23
  55.6 0.8 reshape.160
  56.4 1.8 %bitcast_reduce_fusion = bf16[256,576]{1,0:T(8,128)(2,1)S(1)} fusion(bf16[256,1,576]{2,1,0:T(2,128)(2,1)S(1)} %reshape.160), kind=kLoop, calls=%fused_computation.114 | loop fusion | bytes 589824 | tf_op jit(solution)/shard_map/all_to_all | solution.py:111
  58.3 0.6 reshape.139
  58.8 12.3 %all-gather.4.cloned.1.call-done = bf16[1152,1728]{1,0:T(8,128)(2,1)} async-done(((bf16[72,1728]{1,0:T(8,128)(2,1)}), bf16[1152,1728]{1,0:T(8,128)(2,1)}) %all-gather.4.cloned.1.call-update) | async-done | bytes 3981328 | tf_op jit(solution)/shard_map/all_gather | solution.py:117
  71.2 3.6 %fusion.9 = bf16[16,16,1728]{2,1,0:T(8,128)(2,1)S(1)} fusion(bf16[1152,1728]{1,0:T(8,128)(2,1)} %all-gather.4.cloned.1.call-done, bf16[16,16,1152]{2,1,0:T(8,128)(2,1)S(1)} %constant_dynamic-update-slice_fusion.14, f32[1152]{0:T(1024)S(1)} %broadcast_add_fusion, f32[16,16]{1,0:T(8,128)S(1)} %add_rsqrt_fusion, f32[16,16]{1,0:T(8,128)S(1)} %broadcast_multiply_fusion.2), kind=kOutput, calls=%fused_computation.7 | convolution fusion | flops 1021132800 | bytes 5462528 | tf_op jit(solution)/shard_map/fpd,dc->fpc/dot_general | solution.py:114
  75.0 0.6 reshape.136
  75.5 0.6 reshape.137
  76.1 2.0 %fusion.71 = (f32[16,8,16]{2,1,0:T(8,128)S(1)}, f32[16,8,16,16]{2,3,1,0:T(8,128)}) fusion(bf16[16,16,8,72]{3,2,1,0:T(8,128)(2,1)S(1)} %reshape.136, bf16[16,16,8,72]{3,2,1,0:T(8,128)(2,1)S(1)} %reshape.137), kind=kOutput, calls=%fused_computation.112 | convolution fusion | flops 4816911 | bytes 729088 | tf_op jit(solution)/shard_map/sub | solution.py:37
  78.1 1.7 %fusion.27 = bf16[16,16,8,72]{3,0,2,1:T(8,128)(2,1)S(1)} fusion(bf16[16,16,8,72]{3,2,1,0:T(8,128)(2,1)S(1)} %reshape.139, f32[16,8,16,16]{2,3,1,0:T(8,128)} %get-tuple-element.27, f32[16,8,16]{2,1,0:T(8,128)S(1)} %get-tuple-element.26), kind=kOutput, calls=%fused_computation.37 | convolution fusion | flops 4931584 | bytes 729088 | tf_op jit(solution)/shard_map/bhlm,lbhd->mbhd/dot_general | solution.py:53
  80.4 0.6 reshape.138
  80.9 1.7 %convolution_bitcast_fusion = f32[16,8,16,72]{3,2,1,0:T(8,128)S(1)} fusion(bf16[16,16,8,72]{3,2,1,0:T(8,128)(2,1)S(1)} %reshape.138, f32[16,8,16,16]{2,3,1,0:T(8,128)} %get-tuple-element.27, f32[16,8,16]{2,1,0:T(8,128)} %copy-done.11), kind=kOutput, calls=%fused_computation.23 | convolution fusion | flops 4784128 | bytes 1024000 | tf_op jit(solution)/shard_map/bhlm,mbhd->lbhd/dot_general | solution.py:39
  82.6 0.5 multiply_reduce_fusion.1
  83.2 0.7 copy.63
  83.9 2.0 %fusion.22 = bf16[16,8,16,16]{2,3,1,0:T(8,128)(2,1)S(1)} fusion(f32[16,8,16]{2,1,0:T(8,128)} %copy.63, bf16[16,16,8,72]{3,2,1,0:T(8,128)(2,1)S(1)} %reshape.139, bf16[16,16,8,72]{3,2,1,0:T(8,128)(2,1)S(1)} %reshape.138, f32[16,8,16,16]{2,3,1,0:T(8,128)} %get-tuple-element.27, f32[16,8,16]{2,1,0:T(8,128)} %copy-done.11), kind=kOutput, calls=%fused_computation.28 | convolution fusion | flops 4849664 | bytes 802816 | tf_op jit(solution)/shard_map/lbhd,mbhd->bhlm/dot_general | solution.py:43
  87.9 0.7 concatenate.3
  88.5 3.7 %fusion.68 = (f32[16,16]{1,0:T(8,128)S(1)}, f32[16,16]{1,0:T(8,128)S(1)}, f32[16,16,1152]{2,1,0:T(8,128)S(1)}) fusion(f32[16,16]{1,0:T(8,128)S(1)} %add_rsqrt_fusion, f32[16,16]{1,0:T(8,128)S(1)} %broadcast_multiply_fusion.2, bf16[16,16,1152]{2,1,0:T(8,128)(2,1)S(1)} %constant_dynamic-update-slice_fusion.14, f32[1152]{0:T(1024)S(1)} %copy-done.10, ...), kind=kOutput, calls=%fused_computation.109 | convolution fusion | flops 1021279744 | bytes 6644224 | tf_op jit(solution)/shard_map/fpc,dc->fpd/dot_general | solution.py:122
  92.2 1.2 fusion.35
  93.4 3.8 %all-to-all-start.1 = ((bf16[16,16,1152]{2,1,0:T(8,128)(2,1)}), bf16[16,16,1152]{2,1,0:T(8,128)(2,1)S(1)}, u32[]{:S(2)}, u32[]{:S(2)}) async-start(bf16[16,16,1152]{2,1,0:T(8,128)(2,1)} %fusion.35), calls=%async_computation.1 | async-start | bytes 1179648 | tf_op jit(solution)/shard_map/all_to_all | solution.py:132
  97.3 0.8 fusion.70
  98.0 2.2 %fusion.76 = (f32[8,256]{1,0:T(8,128)S(1)}, f32[8,256,256]{1,2,0:T(8,128)}) fusion(bf16[256,8,72]{0,2,1:T(8,128)(2,1)S(1)} %bitcast.95, bf16[256,8,72]{0,2,1:T(8,128)(2,1)S(1)} %bitcast.97), kind=kOutput, calls=%fused_computation.113 | convolution fusion | flops 77070592 | bytes 2695168 | tf_op jit(solution)/shard_map/sub | solution.py:37
  100.2 1.8 %fusion.38 = bf16[8,256,256]{1,2,0:T(8,128)(2,1)S(1)} fusion(f32[8,256,256]{1,2,0:T(8,128)} %get-tuple-element.30, f32[8,256]{1,0:T(8,128)S(1)} %get-tuple-element.29), kind=kLoop, calls=%fused_computation.54 | loop fusion | flops 1048576 | bytes 3153920 | tf_op jit(solution)/shard_map/convert_element_type | solution.py:38
  102.0 14.7 %all-gather.6.cloned.1.call-done = bf16[16,36,1152]{2,1,0:T(8,128)(2,1)} async-done(((bf16[1,36,1152]{2,1,0:T(8,128)(2,1)}), bf16[16,36,1152]{2,1,0:T(8,128)(2,1)}) %all-gather.6.cloned.1.call-update) | async-done | bytes 1327120 | tf_op jit(solution)/shard_map/all_gather | solution.py:140
  116.8 2.2 %reshape.150 = bf16[576,1152]{1,0:T(8,128)(2,1)S(1)} reshape(bf16[16,36,1152]{2,1,0:T(8,128)(2,1)} %all-gather.6.cloned.1.call-done) | data formatting | bytes 2654208
  119.0 1.2 add_convert_fusion
  120.3 0.6 convolution_convert_fusion.1
  121.2 0.9 copy-done
  123.8 1.0 pad_maximum_fusion
  (80 shorter events, 7.0 us)
Async XLA Ops:
  7.2 1.1 copy-start.4
  7.2 6.1 %copy-start.5 = (bf16[1,256,576]{1,2,0:T(8,128)(2,1)S(1)}, bf16[1,256,576]{1,2,0:T(8,128)(2,1)}, u32[]{:S(2)}) copy-start(bf16[1,256,576]{1,2,0:T(8,128)(2,1)} %param.9) | copy-start | bytes 884740
  7.2 64.0 %all-gather.4.cloned.1.call-start = ((), (), s32[]{:S(2)}) async-start(), calls=%async_computation.2 | async-start | bytes 4386816 | tf_op jit(solution)/shard_map/all_gather | solution.py:117
  8.3 16.9 %collective-permute-start = (bf16[1,16,1152]{2,1,0:T(8,128)(2,1)S(1)}, bf16[1,16,1152]{2,1,0:T(8,128)(2,1)S(1)}, u32[]{:S(2)}, u32[]{:S(2)}) collective-permute-start(bf16[1,16,1152]{2,1,0:T(8,128)(2,1)S(1)} %get-tuple-element.23), channel_id=1, source_target_pairs={{0,1},{1,0},{2,3},{3,2},{4,5},{5,4},{6,7},{7,6},{8,9},{9,8},{10,11... | collective-permute-start | bytes 110600 | tf_op jit(solution)/shard_map/ppermute | solution.py:23
  8.8 19.3 %collective-permute-start.1 = (bf16[1,16,1152]{2,1,0:T(8,128)(2,1)S(1)}, bf16[1,16,1152]{2,1,0:T(8,128)(2,1)S(1)}, u32[]{:S(2)}, u32[]{:S(2)}) collective-permute-start(bf16[1,16,1152]{2,1,0:T(8,128)(2,1)S(1)} %get-tuple-element.22), channel_id=1, source_target_pairs={{0,2},{1,3},{2,0},{3,1},{4,6},{5,7},{6,4},{7,5},{8,10},{9,11},{10,... | collective-permute-start | bytes 110600 | tf_op jit(solution)/shard_map/ppermute | solution.py:23
  11.4 16.8 %collective-permute-start.2 = (bf16[1,16,1152]{2,1,0:T(8,128)(2,1)S(1)}, bf16[1,16,1152]{2,1,0:T(8,128)(2,1)S(1)}, u32[]{:S(2)}, u32[]{:S(2)}) collective-permute-start(bf16[1,16,1152]{2,1,0:T(8,128)(2,1)S(1)} %get-tuple-element.21), channel_id=1, source_target_pairs={{0,3},{1,2},{2,1},{3,0},{4,7},{5,6},{6,5},{7,4},{8,11},{9,10},{10,... | collective-permute-start | bytes 110600 | tf_op jit(solution)/shard_map/ppermute | solution.py:23
  11.5 19.2 %collective-permute-start.3 = (bf16[1,16,1152]{2,1,0:T(8,128)(2,1)S(1)}, bf16[1,16,1152]{2,1,0:T(8,128)(2,1)S(1)}, u32[]{:S(2)}, u32[]{:S(2)}) collective-permute-start(bf16[1,16,1152]{2,1,0:T(8,128)(2,1)S(1)} %get-tuple-element.20), channel_id=1, source_target_pairs={{0,4},{1,5},{2,6},{3,7},{4,0},{5,1},{6,2},{7,3},{8,12},{9,13},{10,... | collective-permute-start | bytes 110600 | tf_op jit(solution)/shard_map/ppermute | solution.py:23
  13.3 17.7 %collective-permute-start.4 = (bf16[1,16,1152]{2,1,0:T(8,128)(2,1)S(1)}, bf16[1,16,1152]{2,1,0:T(8,128)(2,1)S(1)}, u32[]{:S(2)}, u32[]{:S(2)}) collective-permute-start(bf16[1,16,1152]{2,1,0:T(8,128)(2,1)S(1)} %get-tuple-element.19), channel_id=1, source_target_pairs={{0,5},{1,4},{2,7},{3,6},{4,1},{5,0},{6,3},{7,2},{8,13},{9,12},{10,... | collective-permute-start | bytes 110600 | tf_op jit(solution)/shard_map/ppermute | solution.py:23
  13.9 11.2 %copy-start.8 = (f32[1152]{0:T(1024)S(1)}, f32[1152]{0:T(1024)}, u32[]{:S(2)}) copy-start(f32[1152]{0:T(1024)} %param.11) | copy-start | bytes 13828
  18.2 37.5 %all-to-all-start = ((bf16[16,2,4608]{2,1,0:T(2,128)(2,1)}), bf16[16,2,4608]{2,1,0:T(2,128)(2,1)S(1)}, u32[]{:S(2)}, u32[]{:S(2)}) async-start(bf16[16,2,4608]{2,1,0:T(2,128)(2,1)} %reshape.159), calls=%async_computation | async-start | bytes 589824 | tf_op jit(solution)/shard_map/all_to_all | solution.py:111
  24.3 92.5 %all-gather.6.cloned.1.call-start = ((), (), s32[]{:S(2)}) async-start(), calls=%async_computation.3 | async-start | bytes 1566720 | tf_op jit(solution)/shard_map/all_gather | solution.py:140
  25.1 46.1 %copy-start.9 = (f32[1152]{0:T(1024)}, f32[1152]{0:T(1024)S(1)}, u32[]{:S(2)}) copy-start(f32[1152]{0:T(1024)S(1)} %broadcast_add_fusion) | copy-start | bytes 13828
  25.2 11.9 %collective-permute-start.5 = (bf16[1,16,1152]{2,1,0:T(8,128)(2,1)S(1)}, bf16[1,16,1152]{2,1,0:T(8,128)(2,1)S(1)}, u32[]{:S(2)}, u32[]{:S(2)}) collective-permute-start(bf16[1,16,1152]{2,1,0:T(8,128)(2,1)S(1)} %get-tuple-element.18), channel_id=1, source_target_pairs={{0,6},{1,7},{2,4},{3,5},{4,2},{5,3},{6,0},{7,1},{8,14},{9,15},{10,... | collective-permute-start | bytes 110600 | tf_op jit(solution)/shard_map/ppermute | solution.py:23
  28.1 12.4 %collective-permute-start.6 = (bf16[1,16,1152]{2,1,0:T(8,128)(2,1)S(1)}, bf16[1,16,1152]{2,1,0:T(8,128)(2,1)S(1)}, u32[]{:S(2)}, u32[]{:S(2)}) collective-permute-start(bf16[1,16,1152]{2,1,0:T(8,128)(2,1)S(1)} %get-tuple-element.17), channel_id=1, source_target_pairs={{0,7},{1,6},{2,5},{3,4},{4,3},{5,2},{6,1},{7,0},{8,15},{9,14},{10,... | collective-permute-start | bytes 110600 | tf_op jit(solution)/shard_map/ppermute | solution.py:23
  28.2 16.0 %collective-permute-start.7 = (bf16[1,16,1152]{2,1,0:T(8,128)(2,1)S(1)}, bf16[1,16,1152]{2,1,0:T(8,128)(2,1)S(1)}, u32[]{:S(2)}, u32[]{:S(2)}) collective-permute-start(bf16[1,16,1152]{2,1,0:T(8,128)(2,1)S(1)} %get-tuple-element.16), channel_id=1, source_target_pairs={{0,8},{1,9},{2,10},{3,11},{4,12},{5,13},{6,14},{7,15},{8,0},{9,1},... | collective-permute-start | bytes 110600 | tf_op jit(solution)/shard_map/ppermute | solution.py:23
  30.6 14.3 %collective-permute-start.8 = (bf16[1,16,1152]{2,1,0:T(8,128)(2,1)S(1)}, bf16[1,16,1152]{2,1,0:T(8,128)(2,1)S(1)}, u32[]{:S(2)}, u32[]{:S(2)}) collective-permute-start(bf16[1,16,1152]{2,1,0:T(8,128)(2,1)S(1)} %get-tuple-element.15), channel_id=1, source_target_pairs={{0,9},{1,8},{2,11},{3,10},{4,13},{5,12},{6,15},{7,14},{8,1},{9,0},... | collective-permute-start | bytes 110600 | tf_op jit(solution)/shard_map/ppermute | solution.py:23
  31.0 17.2 %collective-permute-start.9 = (bf16[1,16,1152]{2,1,0:T(8,128)(2,1)S(1)}, bf16[1,16,1152]{2,1,0:T(8,128)(2,1)S(1)}, u32[]{:S(2)}, u32[]{:S(2)}) collective-permute-start(bf16[1,16,1152]{2,1,0:T(8,128)(2,1)S(1)} %get-tuple-element.14), channel_id=1, source_target_pairs={{0,10},{1,11},{2,8},{3,9},{4,14},{5,15},{6,12},{7,13},{8,2},{9,3},... | collective-permute-start | bytes 110600 | tf_op jit(solution)/shard_map/ppermute | solution.py:23
  37.1 12.1 %collective-permute-start.10 = (bf16[1,16,1152]{2,1,0:T(8,128)(2,1)S(1)}, bf16[1,16,1152]{2,1,0:T(8,128)(2,1)S(1)}, u32[]{:S(2)}, u32[]{:S(2)}) collective-permute-start(bf16[1,16,1152]{2,1,0:T(8,128)(2,1)S(1)} %get-tuple-element.13), channel_id=1, source_target_pairs={{0,11},{1,10},{2,9},{3,8},{4,15},{5,14},{6,13},{7,12},{8,3},{9,2},... | collective-permute-start | bytes 110600 | tf_op jit(solution)/shard_map/ppermute | solution.py:23
  40.5 8.7 %collective-permute-start.11 = (bf16[1,16,1152]{2,1,0:T(8,128)(2,1)S(1)}, bf16[1,16,1152]{2,1,0:T(8,128)(2,1)S(1)}, u32[]{:S(2)}, u32[]{:S(2)}) collective-permute-start(bf16[1,16,1152]{2,1,0:T(8,128)(2,1)S(1)} %get-tuple-element.12), channel_id=1, source_target_pairs={{0,12},{1,13},{2,14},{3,15},{4,8},{5,9},{6,10},{7,11},{8,4},{9,5},... | collective-permute-start | bytes 110600 | tf_op jit(solution)/shard_map/ppermute | solution.py:23
  44.2 5.3 %collective-permute-start.12 = (bf16[1,16,1152]{2,1,0:T(8,128)(2,1)S(1)}, bf16[1,16,1152]{2,1,0:T(8,128)(2,1)S(1)}, u32[]{:S(2)}, u32[]{:S(2)}) collective-permute-start(bf16[1,16,1152]{2,1,0:T(8,128)(2,1)S(1)} %get-tuple-element.11), channel_id=1, source_target_pairs={{0,13},{1,12},{2,15},{3,14},{4,9},{5,8},{6,11},{7,10},{8,5},{9,4},... | collective-permute-start | bytes 110600 | tf_op jit(solution)/shard_map/ppermute | solution.py:23
  45.0 7.3 %collective-permute-start.13 = (bf16[1,16,1152]{2,1,0:T(8,128)(2,1)S(1)}, bf16[1,16,1152]{2,1,0:T(8,128)(2,1)S(1)}, u32[]{:S(2)}, u32[]{:S(2)}) collective-permute-start(bf16[1,16,1152]{2,1,0:T(8,128)(2,1)S(1)} %get-tuple-element.25), channel_id=1, source_target_pairs={{0,14},{1,15},{2,12},{3,13},{4,10},{5,11},{6,8},{7,9},{8,6},{9,7},... | collective-permute-start | bytes 110600 | tf_op jit(solution)/shard_map/ppermute | solution.py:23
  48.2 7.0 %collective-permute-start.14 = (bf16[1,16,1152]{2,1,0:T(8,128)(2,1)S(1)}, bf16[1,16,1152]{2,1,0:T(8,128)(2,1)S(1)}, u32[]{:S(2)}, u32[]{:S(2)}) collective-permute-start(bf16[1,16,1152]{2,1,0:T(8,128)(2,1)S(1)} %get-tuple-element.10), channel_id=1, source_target_pairs={{0,15},{1,14},{2,13},{3,12},{4,11},{5,10},{6,9},{7,8},{8,7},{9,6},... | collective-permute-start | bytes 110600 | tf_op jit(solution)/shard_map/ppermute | solution.py:23
  78.1 1.8 %copy-start.11 = (f32[16,8,16]{2,1,0:T(8,128)}, f32[16,8,16]{2,1,0:T(8,128)S(1)}, u32[]{:S(2)}) copy-start(f32[16,8,16]{2,1,0:T(8,128)S(1)} %get-tuple-element.26) | copy-start | bytes 24580
  87.5 1.1 copy-start.10
  93.4 3.8 %copy-start.2 = (bf16[3,1,256,576]{2,3,1,0:T(8,128)(2,1)S(1)}, bf16[3,1,256,576]{2,3,1,0:T(8,128)(2,1)}, u32[]{:S(2)}) copy-start(bf16[3,1,256,576]{2,3,1,0:T(8,128)(2,1)} %param.7) | copy-start | bytes 2654212
  93.4 25.6 %all-to-all-start.1 = ((bf16[16,16,1152]{2,1,0:T(8,128)(2,1)}), bf16[16,16,1152]{2,1,0:T(8,128)(2,1)S(1)}, u32[]{:S(2)}, u32[]{:S(2)}) async-start(bf16[16,16,1152]{2,1,0:T(8,128)(2,1)} %fusion.35), calls=%async_computation.1 | async-start | bytes 1179648 | tf_op jit(solution)/shard_map/all_to_all | solution.py:132
  100.2 1.8 %copy-start.6 = (f32[8,256]{1,0:T(8,128)}, f32[8,256]{1,0:T(8,128)S(1)}, u32[]{:S(2)}) copy-start(f32[8,256]{1,0:T(8,128)S(1)} %get-tuple-element.29) | copy-start | bytes 24580
  119.0 1.9 %copy-start.1 = (bf16[1,1,256,576]{2,3,1,0:T(8,128)(2,1)S(1)}, bf16[1,1,256,576]{2,3,1,0:T(8,128)(2,1)}, u32[]{:S(2)}) copy-start(bf16[1,1,256,576]{2,3,1,0:T(8,128)(2,1)} %get-tuple-element.7) | copy-start | bytes 884740
  120.3 1.0 copy-start.3
  120.3 1.8 %copy-start = (f32[8,256,256]{1,2,0:T(8,128)S(1)}, f32[8,256,256]{1,2,0:T(8,128)}, u32[]{:S(2)}) copy-start(f32[8,256,256]{1,2,0:T(8,128)} %get-tuple-element.30) | copy-start | bytes 6291460
  120.9 1.2 copy-start.7
Sparse Core Ops, SparseCore 0:
  10.3 60.7 all-gather.3
  73.3 43.4 all-gather.5
